TPU v7x, 256 devices: a whole 4x4x8 slice. The times are simulated.
256 devices in a mesh: layer: 2 (over x_lo), row: 4 (over x_hi, core), col: 32 (over y, z).
Axes of the slice: x: 4 (x_hi: 2, x_lo: 2; x = x_hi * 2 + x_lo), y: 4, z: 8, core: 2. Of those that a mesh axis runs over, the one named last changes fastest.
Arguments:
- ancestor: float32 [2, 8192, 8192], P('layer', 'row', 'col'), may hold values from -6 to 6
- lower_panels: float32 [2, 4, 512, 8192], P('layer', None, 'col', 'row'), may hold values from -6 to 6
- upper_panels: float32 [2, 4, 512, 8192], P('layer', None, 'row', 'col'), may hold values from -0.25 to 0.25
- lower_blocks: int32 [2, 4, 64], P('layer'), may hold values 0 or 1
- upper_blocks: int32 [2, 4, 64], P('layer'), may hold values 0 or 1
- final_lower: float32 [512, 8192], P(('layer', 'col'), 'row'), may hold values from -6 to 6
- final_upper: float32 [512, 8192], P(('layer', 'row'), 'col'), may hold values from -0.25 to 0.25
- final_lower_blocks: int32 [64], replicated, may hold values 0 or 1
- final_upper_blocks: int32 [64], replicated, may hold values 0 or 1
Outputs:
- summed: float32 [8192, 8192], P('row', 'col')
All inputs are finite; a program needn't handle non-finite values. No bound on the sum of `lower_blocks` or of `upper_blocks` on one device may be relied on, other than what follows from the above.
Results may differ from a plain program's by a relative error of at most 0.0001.
Values sent between devices are 32-bit elements; how exact they have to be, the bound alone decides.
A program may use at most 128 MiB of HBM per device.

v0:
```python
import jax
import jax.numpy as jnp
from jax import lax
from jax.sharding import PartitionSpec as P

BLK = 128
PANELS = 4


def window(blocks, offset, length):
    spread = jnp.repeat(blocks.astype(jnp.float32), BLK, axis=-1)
    return lax.dynamic_slice_in_dim(spread, offset, length, spread.ndim - 1)


def contract(lower_masked, upper_masked):
    return lax.dot_general(
        lower_masked,
        upper_masked,
        (((0,), (0,)), ((), ())),
        precision=lax.Precision.HIGHEST,
        preferred_element_type=jnp.float32,
    )


def body(
    ancestor,
    lower_panels,
    upper_panels,
    lower_blocks,
    upper_blocks,
    final_lower,
    final_upper,
    final_lower_blocks,
    final_upper_blocks,
):
    row_count = ancestor.shape[1]
    col_count = ancestor.shape[2]
    row_start = lax.axis_index("row") * row_count
    col_start = lax.axis_index("col") * col_count
    partial_value = ancestor[0]
    for panel in range(PANELS):
        row_mask = window(lower_blocks[0, panel], row_start, row_count)
        col_mask = window(upper_blocks[0, panel], col_start, col_count)
        upper_full = (
            lax.all_gather(upper_panels[0, panel], "row", axis=0, tiled=True) * col_mask[None, :]
        )

        def subtract(running, lower_piece, offset, upper_full=upper_full, row_mask=row_mask):
            return running - contract(lower_piece * row_mask[None, :], upper_full)

        partial_value = subtract(
            partial_value,
            lax.all_gather(lower_panels[0, panel], "col", axis=0, tiled=True),
            jnp.int32(0),
        )
    final_rows = window(final_lower_blocks, row_start, row_count)
    final_cols = window(final_upper_blocks, col_start, col_count)
    summed = lax.psum(partial_value, "layer")
    final_full = (
        lax.all_gather(final_upper, ("layer", "row"), axis=0, tiled=True) * final_cols[None, :]
    )
    return summed - contract(
        lax.all_gather(final_lower, ("layer", "col"), axis=0, tiled=True) * final_rows[None, :],
        final_full,
    )


def solution(mesh):
    return jax.shard_map(
        body,
        mesh=mesh,
        in_specs=(
            P("layer", "row", "col"),
            P("layer", None, "col", "row"),
            P("layer", None, "row", "col"),
            P("layer", None, None),
            P("layer", None, None),
            P(("layer", "col"), "row"),
            P(("layer", "row"), "col"),
            P(),
            P(),
        ),
        out_specs=P("row", "col"),
        check_vma=False,
    )
```

profile of v0, /device:TPU:4, one launch (start us, length us, event | category | flops | bytes accessed | tf_op | source)
XLA Modules:
  0.0 734.2 jit_solution(1446054610185346086)
XLA Ops:
  6.5 1.9 fusion.25
  8.5 0.7 all-gather.22.cloned.1.call-update
  9.2 0.7 all-gather.16.cloned.1.call-update
  10.0 0.5 all-gather.20.cloned.1.call-update
  10.5 0.5 all-gather.14.cloned.1.call-update
  11.1 0.8 convert_bitcast_fusion.3
  12.1 0.8 convert_bitcast_fusion.2
  13.7 1.1 fusion.24
  14.9 8.3 %all-gather.3 = f32[1,1,512,256]{3,2,1,0:T(8,128)S(1)} all-gather(f32[1,1,128,256]{3,2,1,0:T(8,128)S(1)} %get-tuple-element.6), channel_id=5, replica_groups=mesh['layer'=2,'row'=4,'col'=32] {'row'}, dimensions={2}, use_global_device_ids=true | all-gather | bytes 655360 | tf_op jit(solution)/shard_map/all_gather | solution.py:45
  23.2 8.8 %all-gather.1 = f32[1,1,512,256]{3,2,1,0:T(8,128)S(1)} all-gather(f32[1,1,128,256]{3,2,1,0:T(8,128)S(1)} %get-tuple-element.7), channel_id=3, replica_groups=mesh['layer'=2,'row'=4,'col'=32] {'row'}, dimensions={2}, use_global_device_ids=true | all-gather | bytes 655360 | tf_op jit(solution)/shard_map/all_gather | solution.py:45
  31.9 9.2 %all-gather.7 = f32[1,1,512,256]{3,2,1,0:T(8,128)} all-gather(f32[1,1,128,256]{3,2,1,0:T(8,128)S(1)} %get-tuple-element.8), channel_id=9, replica_groups=mesh['layer'=2,'row'=4,'col'=32] {'row'}, dimensions={2}, use_global_device_ids=true | all-gather | bytes 655360 | tf_op jit(solution)/shard_map/all_gather | solution.py:45
  41.2 8.8 %all-gather.5 = f32[1,1,512,256]{3,2,1,0:T(8,128)S(1)} all-gather(f32[1,1,128,256]{3,2,1,0:T(8,128)S(1)} %get-tuple-element.5), channel_id=7, replica_groups=mesh['layer'=2,'row'=4,'col'=32] {'row'}, dimensions={2}, use_global_device_ids=true | all-gather | bytes 655360 | tf_op jit(solution)/shard_map/all_gather | solution.py:45
  49.9 44.8 %all-gather.18.cloned.1.call-done = f32[1,1,512,2048]{3,2,1,0:T(8,128)} async-done(((f32[1,1,16,2048]{3,2,1,0:T(8,128)}), f32[1,1,512,2048]{3,2,1,0:T(8,128)}) %all-gather.18.cloned.1.call-update) | async-done | bytes 4194320 | tf_op jit(solution)/shard_map/all_gather | solution.py:53
  94.7 10.2 %fusion.2 = f32[2048,256]{1,0:T(8,128)} fusion(f32[1,1,512,2048]{3,2,1,0:T(8,128)} %all-gather.18.cloned.1.call-done, f32[2048]{0:T(1024)S(1)} %dynamic_slice.32, f32[1,1,512,256]{3,2,1,0:T(8,128)S(1)} %all-gather.3, f32[256]{0:T(256)S(1)} %dynamic_slice.33), kind=kOutput, calls=%fused_computation.5 | convolution fusion | flops 3222405120 | bytes 6824960 | tf_op jit(solution)/shard_map/dot_general | solution.py:16
  104.9 71.4 %all-gather.22.cloned.1.call-done = f32[1,1,512,2048]{3,2,1,0:T(8,128)} async-done(((f32[1,1,16,2048]{3,2,1,0:T(8,128)}), f32[1,1,512,2048]{3,2,1,0:T(8,128)}) %all-gather.22.cloned.1.call-update) | async-done | bytes 4194320 | tf_op jit(solution)/shard_map/all_gather | solution.py:53
  176.4 8.8 %fusion = f32[2048,256]{1,0:T(8,128)S(1)} fusion(f32[1,1,512,2048]{3,2,1,0:T(8,128)} %all-gather.22.cloned.1.call-done, f32[2048]{0:T(1024)S(1)} %dynamic_slice.36, f32[1,1,512,256]{3,2,1,0:T(8,128)} %all-gather.7, f32[256]{0:T(256)S(1)} %dynamic_slice.37), kind=kOutput, calls=%fused_computation.1 | convolution fusion | flops 3222405120 | bytes 6824960 | tf_op jit(solution)/shard_map/dot_general | solution.py:16
  185.2 72.9 %all-gather.16.cloned.1.call-done = f32[1,1,512,2048]{3,2,1,0:T(8,128)} async-done(((f32[1,1,16,2048]{3,2,1,0:T(8,128)}), f32[1,1,512,2048]{3,2,1,0:T(8,128)}) %all-gather.16.cloned.1.call-update) | async-done | bytes 4194320 | tf_op jit(solution)/shard_map/all_gather | solution.py:53
  258.0 11.5 %fusion.10 = f32[2048,256]{1,0:T(8,128)} fusion(f32[2048,256]{1,0:T(8,128)} %fusion.2, f32[1,1,512,2048]{3,2,1,0:T(8,128)} %all-gather.16.cloned.1.call-done, f32[1,2048,256]{2,1,0:T(8,128)} %param.9, f32[2048]{0:T(1024)S(1)} %dynamic-slice-done, f32[1,1,512,256]{3,2,1,0:T(8,128)S(1)} %all-gather.1, f32[256]{0:T(256)S(1)} %dynamic_slice.31), kind=kOutput, calls=%fused_computation.12 | convolution fusion | flops 3223453696 | bytes 11019264 | tf_op jit(solution)/shard_map/dot_general | solution.py:16
  269.5 70.0 %all-gather.20.cloned.1.call-done = f32[1,1,512,2048]{3,2,1,0:T(8,128)} async-done(((f32[1,1,16,2048]{3,2,1,0:T(8,128)}), f32[1,1,512,2048]{3,2,1,0:T(8,128)}) %all-gather.20.cloned.1.call-update) | async-done | bytes 4194320 | tf_op jit(solution)/shard_map/all_gather | solution.py:53
  339.6 11.1 %fusion.12 = f32[2048,256]{1,0:T(8,128)} fusion(f32[2048,256]{1,0:T(8,128)S(1)} %fusion, f32[2048,256]{1,0:T(8,128)} %fusion.10, f32[1,1,512,2048]{3,2,1,0:T(8,128)} %all-gather.20.cloned.1.call-done, f32[2048]{0:T(1024)S(1)} %dynamic-slice-done.1, f32[1,1,512,256]{3,2,1,0:T(8,128)S(1)} %all-gather.5, f32[256]{0:T(256)S(1)} %dynamic_slice.35), kind=kOutput, calls=%fused_computation.14 | convolution fusion | flops 3223453696 | bytes 11019264 | tf_op jit(solution)/shard_map/dot_general | solution.py:16
  351.0 14.4 %all_gather.39 = f32[512,256]{1,0:T(8,128)S(1)} all-gather(f32[64,256]{1,0:T(8,128)S(1)} %copy-done), channel_id=1, replica_groups=mesh['layer'=2,'row'=4,'col'=32] {'layer','row'}, dimensions={0}, use_global_device_ids=true | all-gather | bytes 589824 | tf_op jit(solution)/shard_map/all_gather | solution.py:60
  365.4 276.8 %all-gather.14.cloned.1.call-done = f32[512,2048]{1,0:T(8,128)} async-done(((f32[8,2048]{1,0:T(8,128)}), f32[512,2048]{1,0:T(8,128)}) %all-gather.14.cloned.1.call-update) | async-done | bytes 4194320 | tf_op jit(solution)/shard_map/all_gather | solution.py:63
  642.2 74.3 %all-reduce.2.cloned.1.call-done = f32[2048,256]{1,0:T(8,128)} async-done(((f32[2048,256]{1,0:T(8,128)}), f32[2048,256]{1,0:T(8,128)}) %all-reduce.2.cloned.1.call-update) | async-done | bytes 2097168 | tf_op jit(solution)/shard_map/psum | solution.py:58
  716.5 10.9 %fusion.6 = f32[2048,256]{1,0:T(8,128)} fusion(f32[2048,256]{1,0:T(8,128)} %all-reduce.2.cloned.1.call-done, f32[512,2048]{1,0:T(8,128)} %all-gather.14.cloned.1.call-done, f32[2048]{0:T(1024)S(1)} %dynamic_slice.38, f32[512,256]{1,0:T(8,128)S(1)} %all_gather.39, f32[256]{0:T(256)S(1)} %dynamic_slice.39), kind=kOutput, calls=%fused_computation.10 | convolution fusion | flops 3222929408 | bytes 8922112 | tf_op jit(solution)/shard_map/dot_general | solution.py:16
  (42 shorter events, 1.4 us)
Async XLA Ops:
  6.5 88.2 %all-gather.18.cloned.1.call-start = ((), (), s32[]{:S(2)}) async-start(), calls=%async_computation.3 | async-start | bytes 4325376 | tf_op jit(solution)/shard_map/all_gather | solution.py:53
  8.4 167.9 %all-gather.22.cloned.1.call-start = ((), (), s32[]{:S(2)}) async-start(), calls=%async_computation.5 | async-start | bytes 4325376 | tf_op jit(solution)/shard_map/all_gather | solution.py:53
  9.2 248.9 %all-gather.16.cloned.1.call-start = ((), (), s32[]{:S(2)}) async-start(), calls=%async_computation.2 | async-start | bytes 4325376 | tf_op jit(solution)/shard_map/all_gather | solution.py:53
  9.9 329.6 %all-gather.20.cloned.1.call-start = ((), (), s32[]{:S(2)}) async-start(), calls=%async_computation.4 | async-start | bytes 4325376 | tf_op jit(solution)/shard_map/all_gather | solution.py:53
  10.5 631.7 %all-gather.14.cloned.1.call-start = ((), (), s32[]{:S(2)}) async-start(), calls=%async_computation.1 | async-start | bytes 4259840 | tf_op jit(solution)/shard_map/all_gather | solution.py:63
  11.1 705.4 %all-reduce.2.cloned.1.call-start = ((), (), s32[]{:S(2)}) async-start(), calls=%async_computation | async-start | bytes 4194304 | tf_op jit(solution)/shard_map/psum | solution.py:58
  12.1 92.8 %copy-start.1 = (f32[8192]{0:T(1024)}, f32[8192]{0:T(1024)S(1)}, u32[]{:S(2)}) copy-start(f32[8192]{0:T(1024)S(1)} %broadcast_bitcast_fusion.9) | copy-start | bytes 98308
  13.6 91.4 %copy-start.2 = (f32[8192]{0:T(1024)}, f32[8192]{0:T(1024)S(1)}, u32[]{:S(2)}) copy-start(f32[8192]{0:T(1024)S(1)} %broadcast_bitcast_fusion.5) | copy-start | bytes 98308
  176.4 81.7 %dynamic-slice-start = ((f32[8192]{0:T(1024)}, s32[]{:T(128)}), f32[2048]{0:T(1024)S(1)}, s32[]{:S(2)}) async-start(f32[8192]{0:T(1024)} %copy-done.1, s32[]{:T(128)} %select_n.4), calls=%async_computation.6 | async-start | bytes 16896 | tf_op jit(solution)/shard_map/dynamic_slice | solution.py:12
  185.2 154.4 %dynamic-slice-start.1 = ((f32[8192]{0:T(1024)}, s32[]{:T(128)}), f32[2048]{0:T(1024)S(1)}, s32[]{:S(2)}) async-start(f32[8192]{0:T(1024)} %copy-done.2, s32[]{:T(128)} %select_n.4), calls=%async_computation.7 | async-start | bytes 16896 | tf_op jit(solution)/shard_map/dynamic_slice | solution.py:12
  269.5 81.2 %copy-start.3 = (s32[64]{0:T(128)S(1)}, s32[64]{0:T(128)}, u32[]{:S(2)}) copy-start(s32[64]{0:T(128)} %param.16) | copy-start | bytes 772
  269.5 81.3 %copy-start.4 = (s32[64]{0:T(128)S(1)}, s32[64]{0:T(128)}, u32[]{:S(2)}) copy-start(s32[64]{0:T(128)} %param.17) | copy-start | bytes 772
  269.5 81.4 %copy-start = (f32[64,256]{1,0:T(8,128)S(1)}, f32[64,256]{1,0:T(8,128)}, u32[]{:S(2)}) copy-start(f32[64,256]{1,0:T(8,128)} %param.15) | copy-start | bytes 196612
Sparse Core Ops, SparseCore 0:
  9.9 84.7 all-gather.17
  97.3 79.0 all-gather.21
  179.0 79.0 all-gather.15
  260.5 79.0 all-gather.19
  341.2 300.9 all-gather.13
  644.7 71.7 all-reduce.1
where the time goes:
time: 736 us; the launch traced here: 734 us
  waiting for transfers between devices  613 us (83%)
  matrix products  52.5 us (7%)
  blocking collectives  49.5 us (7%)
  between operations  13.5 us (2%)
    all_gather x1, waiting for transfers between devices, body(): lax.all_gather(final_lower, ('layer', 'col'), axis=0, tiled=True)  277 us
    all_gather x4, waiting for transfers between devices, body(): lax.all_gather(lower_panels[0, panel], 'col', axis=0, tiled=True)  259 us
    psum x1, waiting for transfers between devices, body(): summed = lax.psum(partial_value, 'layer')  74.3 us
    dot_general x5, matrix products, contract(): lax.dot_general(lower_masked, upper_masked, (((0,), (0,)), ((), ())), pre...  52.5 us
    all_gather x4, blocking collectives, body(): lax.all_gather(upper_panels[0, panel], 'row', axis=0, tiled=True)  35.1 us
  transfers between devices with their start and end apart: 6, of which 6 were waited for; matrix products, arithmetic and copies ran while one was open for 6% of the time, Pallas kernels for 0%

commit v1 on v0

v1 whole, which is shorter than its diff:
```python
import jax
import jax.numpy as jnp
from jax import lax
from jax.experimental import pallas as pl
from jax.experimental.pallas import tpu as pltpu
from jax.sharding import PartitionSpec as P

BLK = 128
PANELS = 4
NY, NZ = 4, 8
ROWS = 4
R = 2
MESH = pl.DeviceIdType.MESH
F32, BF16 = jnp.float32, jnp.bfloat16


def split(value):
    high = value.astype(BF16)
    return high, (value - high.astype(F32)).astype(BF16)


def contract(lower, upper_high, upper_low):
    high, low = split(lower)

    def dot(a, b):
        return lax.dot_general(a, b, (((0,), (0,)), ((), ())), preferred_element_type=F32)

    return dot(high, upper_high) + dot(high, upper_low) + dot(low, upper_high)


def kernel(
    anc_ref, low_ref, up_ref, lb_ref, ub_ref, fl_ref, fu_ref, flb_ref, fub_ref,
    out_ref,
    ga, gb, ug, uh, ul, fh, flo, anc, mine, rx,
    s_a1, r_a1, s_a2, r_a2, s_b1, r_b1, s_b2, r_b2, s_u, r_u, s_x, r_x, l_anc, l_out,
):
    chunks = ga.shape[0]
    layer = lax.axis_index("layer")
    row = lax.axis_index("row")
    col = lax.axis_index("col")
    y, z = col // NZ, lax.rem(col, NZ)
    sib = row + 1 - 2 * lax.rem(row, 2)
    far = lax.rem(row + 2, ROWS)

    def at_y(d):
        return lax.rem(y + d + NY, NY)

    def at_z(d):
        return lax.rem(z + d + NZ, NZ)

    def col_of(yy, zz):
        return {"col": yy * NZ + zz}

    def remote(ref, ssem, rsem, target):
        return pltpu.make_async_remote_copy(
            src_ref=ref, dst_ref=ref, send_sem=ssem, recv_sem=rsem,
            device_id=target, device_id_type=MESH,
        )

    half_a = {1: (0, 40), -1: (40, 40)}
    half_b = {1: (0, 32), -1: (32, 32)}

    def a1(c, d, h, arriving):
        zz = at_z(-d * (h if arriving else h - 1))
        ref = ga.at[c, y, zz]
        if h == 4:
            ref = ga.at[c, y, zz, pl.ds(*half_a[d]), :]
        k = (0 if d == 1 else 4) + h - 1
        return remote(ref, s_a1.at[c, k], r_a1.at[c, k], col_of(y, at_z(d)))

    def a2(c, d, h, arriving):
        yy = at_y(-d * (h if arriving else h - 1))
        ref = ga.at[c, yy]
        if h == 2:
            ref = ga.at[c, yy, pl.ds(0 if d == 1 else NZ // 2, NZ // 2)]
        k = (0 if d == 1 else 2) + h - 1
        return remote(ref, s_a2.at[c, k], r_a2.at[c, k], col_of(at_y(d), z))

    def b1(c, d, h, arriving):
        yy = at_y(-d * (h if arriving else h - 1))
        ref = gb.at[c, z, yy]
        if h == 2:
            ref = gb.at[c, z, yy, pl.ds(*half_b[d]), :]
        k = (0 if d == 1 else 2) + h - 1
        return remote(ref, s_b1.at[c, k], r_b1.at[c, k], col_of(at_y(d), z))

    def b2(c, d, h, arriving):
        zz = at_z(-d * (h if arriving else h - 1))
        ref = gb.at[c, zz]
        if h == 4:
            ref = gb.at[c, zz, pl.ds(0 if d == 1 else NY // 2, NY // 2)]
        k = (0 if d == 1 else 4) + h - 1
        return remote(ref, s_b2.at[c, k], r_b2.at[c, k], col_of(y, at_z(d)))

    def begin(what, c):
        for d in (1, -1):
            what(c, d, 1, False).start()

    def forward(what, c, h):
        for d in (1, -1):
            what(c, d, h, True).wait_recv()
            what(c, d, h + 1, False).start()

    def arrive(what, c, h):
        for d in (1, -1):
            what(c, d, h, True).wait_recv()

    def sent(what, c, hops):
        for d in (1, -1):
            for h in range(1, hops + 1):
                what(c, d, h, False).wait_send()

    u_own_sib = remote(ug.at[row], s_u.at[0], r_u.at[0], {"row": sib})
    u_own_far = remote(ug.at[row], s_u.at[1], r_u.at[1], {"row": far})
    u_fwd = remote(ug.at[far], s_u.at[2], r_u.at[2], {"row": sib})
    far_sib = lax.rem(sib + 2, ROWS)

    def u_arrive(k, which):
        remote(ug.at[which], s_u.at[k], r_u.at[k], {"row": sib}).wait_recv()

    def exchange(c):
        return pltpu.make_async_remote_copy(
            src_ref=mine.at[c], dst_ref=rx.at[c], send_sem=s_x.at[c], recv_sem=r_x.at[c],
            device_id={"layer": 1 - layer}, device_id_type=MESH,
        )

    def store_out(c):
        return pltpu.make_async_copy(rx.at[c], out_ref.at[c], l_out.at[c])

    load_anc = pltpu.make_async_copy(anc_ref.at[0], anc, l_anc)
    load_anc.start()

    barrier = pltpu.get_barrier_semaphore()
    greeted = [
        {"row": sib}, {"row": far}, {"layer": 1 - layer},
        col_of(at_y(1), z), col_of(at_y(-1), z), col_of(y, at_z(1)), col_of(y, at_z(-1)),
    ]
    for other in greeted:
        pl.semaphore_signal(barrier, inc=1, device_id=other, device_id_type=MESH)

    for panel in range(PANELS):
        ug[row, panel * 128 : panel * 128 + 128, :] = up_ref[0, panel]
    ug[row, PANELS * 128 :, :] = fu_ref[...]

    def place(c, _):
        for r in range(R):
            lanes = pl.ds(pl.multiple_of((c * R + r) * BLK, BLK), BLK)
            for panel in range(PANELS):
                piece = low_ref[0, panel, :, lanes]
                where = pl.ds((panel % 2) * 16 * R + r * 16, 16)
                if panel < 2:
                    ga[c, y, z, where, :] = piece
                else:
                    gb[c, z, y, where, :] = piece
            ga[c, y, z, pl.ds(32 * R + r * 8, 8), :] = fl_ref[:, lanes]
        return 0

    lax.fori_loop(0, chunks, place, 0)
    pl.semaphore_wait(barrier, len(greeted))

    u_own_far.start()
    u_own_sib.start()

    def scale(mask_ref, *index):
        return mask_ref[index].astype(F32)

    def prepare_upper():
        u_arrive(0, sib)
        u_arrive(1, far)
        u_fwd.start()
        u_arrive(2, far_sib)
        for half in range(2):
            cols = slice(half * BLK, half * BLK + BLK)
            for panel in range(PANELS):
                keep = scale(ub_ref, 0, panel, col * 2 + half)
                if panel < 2:
                    for r in range(ROWS):
                        high, low = split(ug[r, panel * 128 : panel * 128 + 128, cols] * keep)
                        uh[panel, r * 128 : r * 128 + 128, cols] = high
                        ul[panel, r * 128 : r * 128 + 128, cols] = low
                else:
                    for source in range(NY * NZ):
                        sy, sz = source // NZ, source % NZ
                        r, at = source // 8, source % 8 * 16
                        to = (sz * NY + sy) * 16
                        high, low = split(
                            ug[r, panel * 128 + at : panel * 128 + at + 16, cols] * keep
                        )
                        uh[panel, to : to + 16, cols] = high
                        ul[panel, to : to + 16, cols] = low
            keep = scale(fub_ref, col * 2 + half)
            for r in range(ROWS):
                high, low = split(ug[r, PANELS * 128 :, cols] * keep)
                fh[r * 64 : r * 64 + 64, cols] = high
                flo[r * 64 : r * 64 + 64, cols] = low

    def compute(c, r):
        block = c * R + r
        rows = pl.ds(pl.multiple_of(block * BLK, BLK), BLK)
        total = anc[rows, :]
        for panel in range(PANELS):
            where = pl.ds((panel % 2) * 16 * R + r * 16, 16)
            held = ga if panel < 2 else gb
            piece = held[c, :, :, where, :].reshape(512, BLK)
            piece = piece * scale(lb_ref, 0, panel, row * 16 + block)
            total = total - contract(piece, uh[panel], ul[panel])
        piece = ga[c, :, :, pl.ds(32 * R + r * 8, 8), :].reshape(256, BLK)
        piece = piece * scale(flb_ref, row * 16 + block)
        total = total - contract(piece, fh[...], flo[...])
        mine[c, r * BLK : r * BLK + BLK, :] = total

    def finish(c):
        exchange(c).wait_recv()
        rx[c] = rx[c] + mine[c]
        store_out(c).start()

    def step(i, _):
        first = i < chunks
        second = (i >= 1) & (i <= chunks)
        third = i >= 2
        j = i - 1
        k = i - 2

        @pl.when(first)
        def _():
            begin(a1, i)
            begin(b1, i)

        @pl.when(second)
        def _():
            begin(a2, j)
            begin(b2, j)

        @pl.when(first)
        def _():
            forward(a1, i, 1)
            forward(b1, i, 1)
            forward(a1, i, 2)
            forward(a1, i, 3)

        @pl.when(i == 0)
        def _():
            load_anc.wait()

        @pl.when(i == 2)
        def _():
            prepare_upper()

        @pl.when(second)
        def _():
            forward(b2, j, 1)

        @pl.when(third)
        def _():
            arrive(a2, k, 2)
            arrive(b2, k, 4)
            compute(k, 0)

        @pl.when(second)
        def _():
            forward(a2, j, 1)
            forward(b2, j, 2)

        @pl.when(third)
        def _():
            compute(k, 1)
            exchange(k).start()
            sent(a1, k, 4)
            sent(b1, k, 2)
            sent(a2, k, 2)
            sent(b2, k, 4)

        @pl.when(second)
        def _():
            forward(b2, j, 3)

        @pl.when(i >= 3)
        def _():
            finish(i - 3)

        @pl.when(first)
        def _():
            arrive(a1, i, 4)
            arrive(b1, i, 2)

        return 0

    lax.fori_loop(0, chunks + 2, step, 0)
    finish(chunks - 1)
    u_own_sib.wait_send()
    u_own_far.wait_send()
    u_fwd.wait_send()

    def drain(c, _):
        exchange(c).wait_send()
        store_out(c).wait()
        return 0

    lax.fori_loop(0, chunks, drain, 0)


def body(anc, low, up, lb, ub, fl, fu, flb, fub):
    rows, cols = anc.shape[1:]
    chunks = rows // BLK // R
    vmem = pl.BlockSpec(memory_space=pltpu.VMEM)
    smem = pl.BlockSpec(memory_space=pltpu.SMEM)
    hbm = pl.BlockSpec(memory_space=pl.ANY)
    dma = pltpu.SemaphoreType.DMA
    out = pl.pallas_call(
        kernel,
        out_shape=jax.ShapeDtypeStruct((chunks, R * BLK, cols), F32),
        in_specs=[hbm, vmem, vmem, smem, smem, vmem, vmem, smem, smem],
        out_specs=hbm,
        scratch_shapes=[
            pltpu.VMEM((chunks, NY, NZ, 40 * R, BLK), F32),
            pltpu.VMEM((chunks, NZ, NY, 32 * R, BLK), F32),
            pltpu.VMEM((ROWS, PANELS * 128 + 64, cols), F32),
            pltpu.VMEM((PANELS, 512, cols), BF16),
            pltpu.VMEM((PANELS, 512, cols), BF16),
            pltpu.VMEM((256, cols), BF16),
            pltpu.VMEM((256, cols), BF16),
            pltpu.VMEM((rows, cols), F32),
            pltpu.VMEM((chunks, R * BLK, cols), F32),
            pltpu.VMEM((chunks, R * BLK, cols), F32),
            dma((chunks, 8)), dma((chunks, 8)),
            dma((chunks, 4)), dma((chunks, 4)),
            dma((chunks, 4)), dma((chunks, 4)),
            dma((chunks, 8)), dma((chunks, 8)),
            dma((3,)), dma((3,)),
            dma((chunks,)), dma((chunks,)),
            dma, dma((chunks,)),
        ],
        compiler_params=pltpu.CompilerParams(
            collective_id=0, has_side_effects=True, vmem_limit_bytes=56 << 20
        ),
        name="gather_update_exchange",
    )(anc, low, up, lb, ub, fl, fu, flb, fub)
    return out.reshape(rows, cols)


def solution(mesh):
    return jax.shard_map(
        body,
        mesh=mesh,
        in_specs=(
            P("layer", "row", "col"),
            P("layer", None, "col", "row"),
            P("layer", None, "row", "col"),
            P("layer", None, None),
            P("layer", None, None),
            P(("layer", "col"), "row"),
            P(("layer", "row"), "col"),
            P(),
            P(),
        ),
        out_specs=P("row", "col"),
        check_vma=False,
    )
```

time: 736 us -> 202 us (0.27)
  waiting for transfers between devices: 613 us -> 0 us
  Pallas kernels: 0 us -> 198 us
  matrix products: 52.5 us -> 0 us
  blocking collectives: 49.5 us -> 0 us
  between operations: 13.5 us -> 0.01 us
    all_gather x5 -> x0, waiting for transfers between devices: 536 us -> none  [the longest x1 277 us: body(): lax.all_gather(final_lower, ('layer', 'col'), axis=0, tiled=True)]
    pallas_call x0 -> x1, Pallas kernels: none -> 198 us  [body(): pl.pallas_call(kernel, out_shape=jax.ShapeDtypeStruct((chunks, R * BLK, c...]
    psum x1 -> x0, waiting for transfers between devices: 74.3 us -> none  [body(): summed = lax.psum(partial_value, 'layer')]
    dot_general x5 -> x0, matrix products: 52.5 us -> none  [contract(): lax.dot_general(lower_masked, upper_masked, (((0,), (0,)), ((), ())), pre...]
    all_gather x5 -> x0, blocking collectives: 49.5 us -> none  [the longest x4 35.1 us: body(): lax.all_gather(upper_panels[0, panel], 'row', axis=0, tiled=True)]
  transfers between devices with their start and end apart: 6 -> 0, of which waited for: 6 -> 0; matrix products, arithmetic and copies ran while one was open for 6% -> 0% of each run, Pallas kernels for 0% -> 0%
where the time goes in v1:
time: 202 us; the launch traced here: 201 us
  Pallas kernels  198 us (98%)
  local copies, waits for them, and re-layouts  3.05 us (2%)
    pallas_call x1, Pallas kernels, body(): pl.pallas_call(kernel, out_shape=jax.ShapeDtypeStruct((chunks, R * BLK, c...  198 us

profile of v1, /device:TPU:4, one launch (start us, length us, event | category | flops | bytes accessed | tf_op | source)
XLA Modules:
  0.0 201.2 jit_solution(797050421298347343)
XLA Ops:
  0.0 198.2 %gather_update_exchange.1 = f32[8,256,256]{2,1,0:T(8,128)} custom-call(f32[1,2048,256]{2,1,0:T(8,128)} %anc_ref.1, f32[1,4,16,2048]{3,2,1,0:T(8,128)} %low_ref.1, f32[1,4,128,256]{3,2,1,0:T(8,128)} %up_ref.1, s32[1,4,64]{2,1,0:T(4,128)} %lb_ref.1, s32[1,4,64]{2,1,0:T(4,128)} %ub_ref.1, f32[8,2048]{1,0:T(8,128)} %fl_ref.1, f32[64,256]{1,0:T(8,128)} %fu_ref.1, ...), custom_call_target="tpu_custom_call" | custom-call | tf_op jit(solution)/shard_map/gather_update_exchange/pallas_call | solution.py:309
  198.2 3.0 %copy.11 = f32[2048,256]{1,0:T(8,128)} copy(f32[2048,256]{1,0:T(8,128)} %bitcast.1) | data formatting | bytes 4194304

commit v2 on v1

--- a/solution.py
+++ b/solution.py
@@ -57,8 +57,8 @@
             device_id=target, device_id_type=MESH,
         )
 
-    half_a = {1: (0, 40), -1: (40, 40)}
-    half_b = {1: (0, 32), -1: (32, 32)}
+    half_a = {1: (0, 40 * R // 16 * 8), -1: (40 * R // 16 * 8, 40 * R - 40 * R // 16 * 8)}
+    half_b = {1: (0, 16 * R), -1: (16 * R, 16 * R)}
 
     def a1(c, d, h, arriving):
         zz = at_z(-d * (h if arriving else h - 1))
@@ -214,79 +214,50 @@
         rx[c] = rx[c] + mine[c]
         store_out(c).start()
 
-    def step(i, _):
-        first = i < chunks
-        second = (i >= 1) & (i <= chunks)
-        third = i >= 2
-        j = i - 1
-        k = i - 2
-
-        @pl.when(first)
-        def _():
-            begin(a1, i)
-            begin(b1, i)
-
-        @pl.when(second)
-        def _():
-            begin(a2, j)
-            begin(b2, j)
-
-        @pl.when(first)
-        def _():
-            forward(a1, i, 1)
-            forward(b1, i, 1)
-            forward(a1, i, 2)
-            forward(a1, i, 3)
-
-        @pl.when(i == 0)
+    def upper(c):
+        @pl.when(c == 0)
         def _():
             load_anc.wait()
-
-        @pl.when(i == 2)
-        def _():
             prepare_upper()
 
-        @pl.when(second)
-        def _():
-            forward(b2, j, 1)
-
-        @pl.when(third)
-        def _():
-            arrive(a2, k, 2)
-            arrive(b2, k, 4)
-            compute(k, 0)
-
-        @pl.when(second)
-        def _():
-            forward(a2, j, 1)
-            forward(b2, j, 2)
-
-        @pl.when(third)
-        def _():
-            compute(k, 1)
-            exchange(k).start()
-            sent(a1, k, 4)
-            sent(b1, k, 2)
-            sent(a2, k, 2)
-            sent(b2, k, 4)
-
-        @pl.when(second)
-        def _():
-            forward(b2, j, 3)
-
-        @pl.when(i >= 3)
-        def _():
-            finish(i - 3)
-
-        @pl.when(first)
-        def _():
-            arrive(a1, i, 4)
-            arrive(b1, i, 2)
-
+    def work(c):
+        for r in range(R):
+            compute(c, r)
+        exchange(c).start()
+
+    def clear(c):
+        sent(a1, c, 4)
+        sent(b1, c, 2)
+        sent(a2, c, 2)
+        sent(b2, c, 4)
+
+    def starts(what):
+        return lambda c: begin(what, c)
+
+    def moves(what, hop):
+        return lambda c: forward(what, c, hop)
+
+    def ends(what, hop):
+        return lambda c: arrive(what, c, hop)
+
+    def step(i, _):
+        def run(offset, *actions):
+            @pl.when((i >= offset) & (i < chunks + offset))
+            def _():
+                for action in actions:
+                    action(i - offset)
+
+        run(0, starts(a1), starts(b1))
+        run(1, moves(a1, 1), moves(b1, 1))
+        run(2, moves(a1, 2), ends(b1, 2), starts(b2))
+        run(3, moves(a1, 3), moves(b2, 1))
+        run(4, ends(a1, 4), starts(a2), moves(b2, 2))
+        run(5, moves(a2, 1), moves(b2, 3))
+        run(6, upper, ends(a2, 2), ends(b2, 4), work)
+        run(7, clear, finish)
         return 0
 
-    lax.fori_loop(0, chunks + 2, step, 0)
-    finish(chunks - 1)
+    lax.fori_loop(0, chunks + 8, step, 0)
     u_own_sib.wait_send()
     u_own_far.wait_send()
     u_fwd.wait_send()

time: 202 us -> 137 us (0.68)
  Pallas kernels: 198 us -> 134 us
    pallas_call x1, Pallas kernels: 198 us -> 134 us  [body(): pl.pallas_call(kernel, out_shape=jax.ShapeDtypeStruct((chunks, R * BLK, c...]
where the time goes in v2:
time: 137 us
  Pallas kernels  134 us (98%)
  local copies, waits for them, and re-layouts  3.05 us (2%)
    pallas_call x1, Pallas kernels, body(): pl.pallas_call(kernel, out_shape=jax.ShapeDtypeStruct((chunks, R * BLK, c...  134 us
    unnamed x1, local copies, waits for them, and re-layouts  3.05 us

profile of v2, /device:TPU:4, one launch (start us, length us, event | category | flops | bytes accessed | tf_op | source)
XLA Modules:
  0.0 136.7 jit_solution(16276227395648478585)
XLA Ops:
  0.0 133.7 %gather_update_exchange.1 = f32[8,256,256]{2,1,0:T(8,128)} custom-call(f32[1,2048,256]{2,1,0:T(8,128)} %anc_ref.1, f32[1,4,16,2048]{3,2,1,0:T(8,128)} %low_ref.1, f32[1,4,128,256]{3,2,1,0:T(8,128)} %up_ref.1, s32[1,4,64]{2,1,0:T(4,128)} %lb_ref.1, s32[1,4,64]{2,1,0:T(4,128)} %ub_ref.1, f32[8,2048]{1,0:T(8,128)} %fl_ref.1, f32[64,256]{1,0:T(8,128)} %fu_ref.1, ...), custom_call_target="tpu_custom_call" | custom-call | tf_op jit(solution)/shard_map/gather_update_exchange/pallas_call | solution.py:280
  133.7 3.0 %copy.11 = f32[2048,256]{1,0:T(8,128)} copy(f32[2048,256]{1,0:T(8,128)} %bitcast.1) | data formatting | bytes 4194304

commit v3 on v2

v3 whole, which is shorter than its diff:
```python
import functools

import jax
import jax.numpy as jnp
from jax import lax
from jax.experimental import pallas as pl
from jax.experimental.pallas import tpu as pltpu
from jax.sharding import PartitionSpec as P

BLK = 128
PANELS = 4
NY, NZ = 4, 8
ROWS = 4
R = 2
CHUNKS = 8
TILES = 9
BLOCKS = 16
SIZES = ((11, 7), (12, 7), (18, 11))
T_OF, ORDER, SOURCE, POS, POS_OTHER, MOST = 0, 9, 10, 12, 13, 14
MESH = pl.DeviceIdType.MESH
F32, BF16 = jnp.float32, jnp.bfloat16


def split(value):
    high = value.astype(BF16)
    return high, (value - high.astype(F32)).astype(BF16)


def contract(high, low, upper_high, upper_low):

    def dot(a, b):
        return lax.dot_general(a, b, (((0,), (0,)), ((), ())), preferred_element_type=F32)

    return dot(high, upper_high) + dot(high, upper_low) + dot(low, upper_high)


def kernel(
    tiles, tiles_a, tab_ref, anc_ref, low_ref, up_ref, ub_ref, fl_ref, fu_ref, fub_ref,
    mine_ref, rx_ref,
    gathered, own, high, low, ug, uh, ul, anc, mine,
    s_a1, r_a1, s_a2, r_a2, s_b1, r_b1, s_b2, r_b2, s_u, r_u, s_x, r_x, l_anc, l_out,
):
    chunks = CHUNKS
    tiles_b = tiles - tiles_a
    layer = lax.axis_index("layer")
    row = lax.axis_index("row")
    col = lax.axis_index("col")
    y, z = col // NZ, lax.rem(col, NZ)
    sib = row + 1 - 2 * lax.rem(row, 2)
    far = lax.rem(row + 2, ROWS)

    def at_y(d):
        return lax.rem(y + d + NY, NY)

    def at_z(d):
        return lax.rem(z + d + NZ, NZ)

    def col_of(yy, zz):
        return {"col": yy * NZ + zz}

    def remote(ref, ssem, rsem, target):
        return pltpu.make_async_remote_copy(
            src_ref=ref, dst_ref=ref, send_sem=ssem, recv_sem=rsem,
            device_id=target, device_id_type=MESH,
        )

    def halved(d, first, count):
        cut = count // 2
        return (first, cut) if d == 1 else (first + cut, count - cut)

    def part(yy, zz, c, first, count):
        return gathered.at[yy, zz, pl.ds((c * tiles + first) * 8, count * 8), :]

    def a1(c, d, h, arriving):
        zz = at_z(-d * (h if arriving else h - 1))
        span = halved(d, 0, tiles_a) if h == 4 else (0, tiles_a)
        k = (0 if d == 1 else 4) + h - 1
        return remote(part(y, zz, c, *span), s_a1.at[c, k], r_a1.at[c, k], col_of(y, at_z(d)))

    def a2(c, d, h, arriving):
        yy = at_y(-d * (h if arriving else h - 1))
        zz = pl.ds(*(halved(d, 0, NZ) if h == 2 else (0, NZ)))
        k = (0 if d == 1 else 2) + h - 1
        return remote(
            part(yy, zz, c, 0, tiles_a), s_a2.at[c, k], r_a2.at[c, k], col_of(at_y(d), z)
        )

    def b1(c, d, h, arriving):
        yy = at_y(-d * (h if arriving else h - 1))
        span = halved(d, tiles_a, tiles_b) if h == 2 else (tiles_a, tiles_b)
        k = (0 if d == 1 else 2) + h - 1
        return remote(part(yy, z, c, *span), s_b1.at[c, k], r_b1.at[c, k], col_of(at_y(d), z))

    def b2(c, d, h, arriving):
        zz = at_z(-d * (h if arriving else h - 1))
        yy = pl.ds(*(halved(d, 0, NY) if h == 4 else (0, NY)))
        k = (0 if d == 1 else 4) + h - 1
        return remote(
            part(yy, zz, c, tiles_a, tiles_b), s_b2.at[c, k], r_b2.at[c, k], col_of(y, at_z(d))
        )

    def begin(what, c):
        for d in (1, -1):
            what(c, d, 1, False).start()

    def forward(what, c, h):
        for d in (1, -1):
            what(c, d, h, True).wait_recv()
            what(c, d, h + 1, False).start()

    def arrive(what, c, h):
        for d in (1, -1):
            what(c, d, h, True).wait_recv()

    def sent(what, c, hops):
        for d in (1, -1):
            for h in range(1, hops + 1):
                what(c, d, h, False).wait_send()

    u_own_sib = remote(ug.at[row], s_u.at[0], r_u.at[0], {"row": sib})
    u_own_far = remote(ug.at[row], s_u.at[1], r_u.at[1], {"row": far})
    u_fwd = remote(ug.at[far], s_u.at[2], r_u.at[2], {"row": sib})
    far_sib = lax.rem(sib + 2, ROWS)

    def u_arrive(k, which):
        remote(ug.at[which], s_u.at[k], r_u.at[k], {"row": sib}).wait_recv()

    def exchange(c):
        return pltpu.make_async_remote_copy(
            src_ref=mine.at[c], dst_ref=rx_ref.at[c], send_sem=s_x.at[c], recv_sem=r_x.at[c],
            device_id={"layer": 1 - layer}, device_id_type=MESH,
        )

    def store_out(c):
        return pltpu.make_async_copy(mine.at[c], mine_ref.at[c], l_out.at[c])

    load_anc = pltpu.make_async_copy(anc_ref, anc, l_anc)
    load_anc.start()

    barrier = pltpu.get_barrier_semaphore()
    greeted = [
        {"row": sib}, {"row": far}, {"layer": 1 - layer},
        col_of(at_y(1), z), col_of(at_y(-1), z), col_of(y, at_z(1)), col_of(y, at_z(-1)),
    ]
    for other in greeted:
        pl.semaphore_signal(barrier, inc=1, device_id=other, device_id_type=MESH)

    for panel in range(PANELS):
        ug[row, panel * 128 : panel * 128 + 128, :] = up_ref[0, panel]
    ug[row, PANELS * 128 :, :] = fu_ref[...]

    for r in range(BLOCKS):
        lanes = slice(r * BLK, r * BLK + BLK)
        for q in range(TILES - 1):
            own[r * TILES + q] = low_ref[q, :, lanes]
        own[r * TILES + TILES - 1] = fl_ref[:, lanes]
    high[0] = jnp.zeros(high.shape[1:], BF16)
    low[0] = jnp.zeros(low.shape[1:], BF16)

    def place(c):
        for n in range(tiles):
            t = c * tiles + n
            gathered[y, z, pl.ds(t * 8, 8), :] = own[tab_ref[SOURCE + t // BLK, lax.rem(t, BLK)]]

    def unpack(c):
        for n in range(tiles):
            t = c * tiles + n
            piece = gathered[:, :, pl.ds(t * 8, 8), :].reshape(256, BLK)
            high[t + 1], low[t + 1] = split(piece)

    pl.semaphore_wait(barrier, len(greeted))

    u_own_far.start()
    u_own_sib.start()

    def scale(mask_ref, *index):
        return mask_ref[index].astype(F32)

    def prepare_upper():
        u_arrive(0, sib)
        u_arrive(1, far)
        u_fwd.start()
        u_arrive(2, far_sib)
        for half in range(2):
            cols = slice(half * BLK, half * BLK + BLK)
            for panel in range(PANELS):
                keep = scale(ub_ref, 0, panel, col * 2 + half)
                for odd in range(2):
                    for pair in range(NY * NZ // 2):
                        r, at = pair // 4, panel * 128 + pair % 4 * 32 + odd * 8
                        both = jnp.concatenate(
                            [ug[r, at : at + 8, cols], ug[r, at + 16 : at + 24, cols]], axis=0
                        )
                        above, below = split(both * keep)
                        to = slice(pair * 16, pair * 16 + 16)
                        uh[panel * 2 + odd, to, cols] = above
                        ul[panel * 2 + odd, to, cols] = below
            keep = scale(fub_ref, col * 2 + half)
            for r in range(ROWS):
                above, below = split(ug[r, PANELS * 128 :, cols] * keep)
                uh[TILES - 1, r * 64 : r * 64 + 64, cols] = above
                ul[TILES - 1, r * 64 : r * 64 + 64, cols] = below

    def compute(c, r):
        at = row * BLOCKS + c * R + r
        total = anc[tab_ref[ORDER, at]]
        for q in range(TILES):
            t = tab_ref[T_OF + q, at]
            total = total - contract(high[t], low[t], uh[q], ul[q])
        mine[c, r * BLK : r * BLK + BLK, :] = total

    def upper(c):
        @pl.when(c == 0)
        def _():
            load_anc.wait()
            prepare_upper()

    def work(c):
        unpack(c)
        for r in range(R):
            compute(c, r)
        exchange(c).start()
        store_out(c).start()

    def clear(c):
        sent(a1, c, 4)
        sent(b1, c, 2)
        sent(a2, c, 2)
        sent(b2, c, 4)

    def starts(what):
        return lambda c: begin(what, c)

    def moves(what, hop):
        return lambda c: forward(what, c, hop)

    def ends(what, hop):
        return lambda c: arrive(what, c, hop)

    def step(i, _):
        def run(offset, *actions):
            @pl.when((i >= offset) & (i < chunks + offset))
            def _():
                for action in actions:
                    action(i - offset)

        run(0, place, starts(a1), starts(b1))
        run(1, moves(a1, 1), moves(b1, 1))
        run(2, moves(a1, 2), ends(b1, 2), starts(b2))
        run(3, moves(a1, 3), moves(b2, 1))
        run(4, ends(a1, 4), starts(a2), moves(b2, 2))
        run(5, moves(a2, 1), moves(b2, 3))
        run(6, upper, ends(a2, 2), ends(b2, 4), work)
        run(7, clear)
        return 0

    lax.fori_loop(0, chunks + 8, step, 0)
    u_own_sib.wait_send()
    u_own_far.wait_send()
    u_fwd.wait_send()

    def drain(c, _):
        exchange(c).wait()
        store_out(c).wait()
        return 0

    lax.fori_loop(0, chunks, drain, 0)


def tables(lb_ref, flb_ref, tab_ref, mask, other, sent, came):
    layer = lax.axis_index("layer")
    row = lax.axis_index("row")
    barrier = pltpu.get_barrier_semaphore()
    target = {"layer": 1 - layer}
    pl.semaphore_signal(barrier, inc=1, device_id=target, device_id_type=MESH)
    mask[...] = jnp.zeros_like(mask)
    mask[0:PANELS, 0:64] = lb_ref[0].astype(F32)
    mask[PANELS : PANELS + 1, 0:64] = flb_ref[...].astype(F32)
    pl.semaphore_wait(barrier, 1)
    copy = pltpu.make_async_remote_copy(
        src_ref=mask, dst_ref=other, send_sem=sent, recv_sem=came,
        device_id=target, device_id_type=MESH,
    )
    copy.start()
    square = (BLK, BLK)
    sub = lax.broadcasted_iota(jnp.int32, square, 0)
    lane = lax.broadcasted_iota(jnp.int32, square, 1)
    same = ((sub >> 4) == (lane >> 4)).astype(F32)
    earlier = (sub < lane).astype(F32)

    def ranked(held):
        weight = 2.0 * jnp.sum(held[0:PANELS], axis=0, keepdims=True) + held[PANELS : PANELS + 1]
        here = jnp.broadcast_to(weight, square)
        there = here.T
        before = jnp.where(there < here, 1.0, jnp.where(there == here, earlier, 0.0)) * same
        place = jnp.sum(before, axis=0, keepdims=True)
        start = jnp.sum(before * there, axis=0, keepdims=True)
        most = jnp.max(jnp.sum(same * there, axis=0, keepdims=True), axis=1, keepdims=True)
        return place, start, most

    held = mask[...]
    place, start, most = ranked(held)
    has = [held[min(q // 2, PANELS) : min(q // 2, PANELS) + 1] for q in range(TILES)]
    spots = []
    for q in range(TILES):
        spots.append(start)
        start = start + has[q]
    ours = ((lax.broadcasted_iota(jnp.int32, (1, BLK), 1) >> 4) == row).astype(F32)
    rows = [h * ours * (spot + 1.0) - 1.0 for h, spot in zip(has, spots)] + [place]
    turned = jnp.concatenate(rows + [jnp.zeros((BLK - TILES - 1, BLK), F32)], axis=0).T
    lane_f = lane.astype(F32)
    within = (sub & 15).astype(F32)
    hit = jnp.where(turned[:, TILES : TILES + 1] == (lane & 15).astype(F32), same, 0.0)
    source = [jnp.zeros(square, F32) for _ in range(2)]
    for q in range(TILES):
        spot = turned[:, q : q + 1]
        code = within * float(TILES) + float(q)
        for part in range(2):
            source[part] = source[part] + jnp.where(spot == lane_f + float(part * BLK), code, 0.0)
    moved = [h * (spot + 1.0) for h, spot in zip(has, spots)]
    moved.append((lax.broadcasted_iota(jnp.int32, (1, BLK), 1) & 15).astype(F32))
    moved = jnp.concatenate(moved + [jnp.zeros((16 - len(moved), BLK), F32)], axis=0)
    moved = jnp.dot(moved, hit, precision=lax.Precision.HIGHEST, preferred_element_type=F32)
    out = [jnp.sum(value, axis=0, keepdims=True) for value in source]
    out.append(place)
    copy.wait()
    place_other, _, most_other = ranked(other[...])
    out.append(place_other)
    out.append(jnp.broadcast_to(jnp.maximum(most, most_other), (1, BLK)))
    tab_ref[0:TILES + 1, :] = (moved[0:TILES + 1] + 0.5).astype(jnp.int32)
    for n, value in enumerate(out):
        tab_ref[SOURCE + n : SOURCE + n + 1, :] = value.astype(jnp.int32)
    tab_ref[MOST + 1 :, :] = jnp.zeros((16 - MOST - 1, BLK), jnp.int32)


def combine(tab_ref, mine_ref, rx_ref, out_ref, mine, rx, total, sem_m, sem_r, sem_o):
    row = lax.axis_index("row")

    def loads(n):
        at = row * BLOCKS + n
        return (
            pltpu.make_async_copy(mine_ref.at[tab_ref[POS, at]], mine.at[n], sem_m.at[n]),
            pltpu.make_async_copy(rx_ref.at[tab_ref[POS_OTHER, at]], rx.at[n], sem_r.at[n]),
        )

    def store(n):
        return pltpu.make_async_copy(total.at[n], out_ref.at[n], sem_o.at[n])

    for n in range(BLOCKS):
        for load in loads(n):
            load.start()
    for n in range(BLOCKS):
        for load in loads(n):
            load.wait()
        total[n] = mine[n] + rx[n]
        store(n).start()
    for n in range(BLOCKS):
        store(n).wait()


VMEM = pl.BlockSpec(memory_space=pltpu.VMEM)
SMEM = pl.BlockSpec(memory_space=pltpu.SMEM)
HBM = pl.BlockSpec(memory_space=pl.ANY)


def gather_update(n, cols, rows):
    tiles, tiles_a = SIZES[n]
    dma = pltpu.SemaphoreType.DMA
    result = jax.ShapeDtypeStruct((CHUNKS, R * BLK, cols), F32)
    return pl.pallas_call(
        functools.partial(kernel, tiles, tiles_a),
        out_shape=(result, result),
        in_specs=[SMEM, HBM, VMEM, VMEM, SMEM, VMEM, VMEM, SMEM],
        out_specs=(HBM, HBM),
        scratch_shapes=[
            pltpu.VMEM((NY, NZ, CHUNKS * tiles * 8, BLK), F32),
            pltpu.VMEM((BLOCKS * TILES, 8, BLK), F32),
            pltpu.VMEM((CHUNKS * tiles + 1, 256, BLK), BF16),
            pltpu.VMEM((CHUNKS * tiles + 1, 256, BLK), BF16),
            pltpu.VMEM((ROWS, PANELS * 128 + 64, cols), F32),
            pltpu.VMEM((TILES, 256, cols), BF16),
            pltpu.VMEM((TILES, 256, cols), BF16),
            pltpu.VMEM((BLOCKS, BLK, cols), F32),
            pltpu.VMEM((CHUNKS, R * BLK, cols), F32),
            dma((CHUNKS, 8)), dma((CHUNKS, 8)),
            dma((CHUNKS, 4)), dma((CHUNKS, 4)),
            dma((CHUNKS, 4)), dma((CHUNKS, 4)),
            dma((CHUNKS, 8)), dma((CHUNKS, 8)),
            dma((3,)), dma((3,)),
            dma((CHUNKS,)), dma((CHUNKS,)),
            dma, dma((CHUNKS,)),
        ],
        compiler_params=pltpu.CompilerParams(
            collective_id=n + 1, has_side_effects=True, vmem_limit_bytes=56 << 20
        ),
        name="gather_update_exchange",
    )


def body(anc, low, up, lb, ub, fl, fu, flb, fub):
    rows, cols = anc.shape[1:]
    dma = pltpu.SemaphoreType.DMA
    tab = pl.pallas_call(
        tables,
        out_shape=jax.ShapeDtypeStruct((16, BLK), jnp.int32),
        in_specs=[VMEM, VMEM],
        out_specs=VMEM,
        scratch_shapes=[pltpu.VMEM((8, BLK), F32), pltpu.VMEM((8, BLK), F32), dma, dma],
        compiler_params=pltpu.CompilerParams(collective_id=0, has_side_effects=True),
        name="block_tables",
    )(lb, flb.reshape(1, -1))
    most = tab[MOST, 0]
    size = sum((most > tiles * CHUNKS).astype(jnp.int32) for tiles, _ in SIZES[:-1])
    mine, rx = lax.switch(
        size,
        [gather_update(n, cols, rows) for n in range(len(SIZES))],
        tab, anc.reshape(BLOCKS, BLK, cols), low.reshape(2 * PANELS, 8, rows), up, ub, fl, fu, fub,
    )
    blocks = (BLOCKS, BLK, cols)
    out = pl.pallas_call(
        combine,
        out_shape=jax.ShapeDtypeStruct(blocks, F32),
        in_specs=[SMEM, HBM, HBM],
        out_specs=HBM,
        scratch_shapes=[pltpu.VMEM(blocks, F32)] * 3 + [dma((BLOCKS,))] * 3,
        compiler_params=pltpu.CompilerParams(vmem_limit_bytes=16 << 20),
        name="layer_sum",
    )(tab, mine.reshape(blocks), rx.reshape(blocks))
    return out.reshape(rows, cols)


def solution(mesh):
    return jax.shard_map(
        body,
        mesh=mesh,
        in_specs=(
            P("layer", "row", "col"),
            P("layer", None, "col", "row"),
            P("layer", None, "row", "col"),
            P("layer", None, None),
            P("layer", None, None),
            P(("layer", "col"), "row"),
            P(("layer", "row"), "col"),
            P(),
            P(),
        ),
        out_specs=P("row", "col"),
        check_vma=False,
    )
```

time: 137 us -> 116 us (0.85)
  Pallas kernels: 134 us -> 113 us
  local copies, waits for them, and re-layouts: 3.05 us -> 0.51 us
    pallas_call x1 -> x3, Pallas kernels: 134 us -> 113 us  [the longest x1 100 us: body(): lax.switch(size, [gather_update(n, cols, rows) for n in range(len(SIZES))...]
    unnamed x1 -> x0, local copies, waits for them, and re-layouts: 3.05 us -> none
where the time goes in v3:
time: 116 us; the launch traced here: 114 us
  Pallas kernels  113 us (97%)
  between operations  1.32 us (1%)
    pallas_call x1, Pallas kernels, body(): lax.switch(size, [gather_update(n, cols, rows) for n in range(len(SIZES))...  100 us
    pallas_call x1, Pallas kernels, body(): pl.pallas_call(combine, out_shape=jax.ShapeDtypeStruct(blocks, F32), in_s...  7.92 us
    pallas_call x1, Pallas kernels, body(): pl.pallas_call(tables, out_shape=jax.ShapeDtypeStruct((16, BLK), jnp.int3...  4.51 us

profile of v3, /device:TPU:4, one launch (start us, length us, event | category | flops | bytes accessed | tf_op | source)
XLA Modules:
  0.0 114.5 jit_solution(1407360849694410754)
XLA Ops:
  0.0 4.5 %block_tables.1.tab_ref = s32[16,128]{1,0:T(8,128)S(1)} custom-call(s32[1,4,64]{2,1,0:T(4,128)} %lb_ref.1, s32[1,64]{1,0:T(1,128)} %bitcast.23), custom_call_target="tpu_custom_call" | custom-call | tf_op jit(solution)/shard_map/block_tables/pallas_call | solution.py:403
  4.5 0.5 slice.3
  6.3 100.2 %conditional.1 = (f32[16,128,256]{2,1,0:T(8,128)S(1)}, f32[16,128,256]{2,1,0:T(8,128)S(1)}) conditional(s32[]{:T(128)} %bitcast.7, (s32[16,128]{1,0:T(8,128)S(1)}, f32[16,128,256]{2,1,0:T(8,128)}, f32[8,8,2048]{2,1,0:T(8,128)}, f32[1,4,128,256]{3,2,1,0:T(8,128)}, s32[1,4,64]{2,1,0:T(4,128)}, /*index=5*/f32[8,2048]{1,0:T(8,128)}, ...), branch_computations={%region_0.0_spmd, %region_1.0_spmd, %region_2.0_spmd} | conditional | bytes 16 | solution.py:414
  6.3 100.2 %gather_update_exchange.3 = (f32[8,256,256]{2,1,0:T(8,128)S(1)}, f32[8,256,256]{2,1,0:T(8,128)S(1)}) custom-call(s32[16,128]{1,0:T(8,128)S(1)} %get-tuple-element.61.tab_ref, f32[16,128,256]{2,1,0:T(8,128)} %get-tuple-element.62.anc_ref, f32[8,8,2048]{2,1,0:T(8,128)} %get-tuple-element.63.low_ref, f32[1,4,128,256]{3,2,1,0:T(8,128)} %get-tuple-element.64.up_ref, ...), custom_call_target="tpu_custom_call" | custom-call | tf_op jit(solution)/shard_map/cond/branch_0_fun/gather_update_exchange/pallas_call | solution.py:414
  106.6 7.9 %layer_sum.1 = f32[16,128,256]{2,1,0:T(8,128)} custom-call(s32[16,128]{1,0:T(8,128)S(1)} %block_tables.1.tab_ref, f32[16,128,256]{2,1,0:T(8,128)S(1)} %get-tuple-element.93.mine_ref, f32[16,128,256]{2,1,0:T(8,128)S(1)} %get-tuple-element.94.rx_ref), custom_call_target="tpu_custom_call" | custom-call | tf_op jit(solution)/shard_map/layer_sum/pallas_call | solution.py:420

commit v4 on v3

--- a/solution.py
+++ b/solution.py
@@ -77,13 +77,45 @@
         k = (0 if d == 1 else 4) + h - 1
         return remote(part(y, zz, c, *span), s_a1.at[c, k], r_a1.at[c, k], col_of(y, at_z(d)))
 
-    def a2(c, d, h, arriving):
-        yy = at_y(-d * (h if arriving else h - 1))
-        zz = pl.ds(*(halved(d, 0, NZ) if h == 2 else (0, NZ)))
-        k = (0 if d == 1 else 2) + h - 1
+    def line(c, d, far_z, arriving):
+        yy = at_y(-d if arriving else 0)
+        zz = at_z(far_z)
+        k = (0 if d == 1 else NZ + 1) + far_z % NZ
         return remote(
             part(yy, zz, c, 0, tiles_a), s_a2.at[c, k], r_a2.at[c, k], col_of(at_y(d), z)
         )
+
+    def onward(c, d, arriving):
+        yy = at_y(-d * (2 if arriving else 1))
+        zz = pl.ds(*halved(d, 0, NZ))
+        k = (0 if d == 1 else NZ + 1) + NZ
+        return remote(
+            part(yy, zz, c, 0, tiles_a), s_a2.at[c, k], r_a2.at[c, k], col_of(at_y(d), z)
+        )
+
+    def spread(*far_z):
+        def act(c):
+            for k in far_z:
+                for d in (1, -1):
+                    line(c, d, k, False).start()
+
+        return act
+
+    def a2_on(c):
+        for d in (1, -1):
+            for k in range(NZ):
+                line(c, d, k, True).wait_recv()
+            onward(c, d, False).start()
+
+    def a2_end(c):
+        for d in (1, -1):
+            onward(c, d, True).wait_recv()
+
+    def a2_sent(c):
+        for d in (1, -1):
+            for k in range(NZ):
+                line(c, d, k, False).wait_send()
+            onward(c, d, False).wait_send()
 
     def b1(c, d, h, arriving):
         yy = at_y(-d * (h if arriving else h - 1))
@@ -176,30 +208,26 @@
     def scale(mask_ref, *index):
         return mask_ref[index].astype(F32)
 
-    def prepare_upper():
-        u_arrive(0, sib)
-        u_arrive(1, far)
-        u_fwd.start()
-        u_arrive(2, far_sib)
+    def convert_upper(r):
         for half in range(2):
             cols = slice(half * BLK, half * BLK + BLK)
             for panel in range(PANELS):
                 keep = scale(ub_ref, 0, panel, col * 2 + half)
                 for odd in range(2):
-                    for pair in range(NY * NZ // 2):
-                        r, at = pair // 4, panel * 128 + pair % 4 * 32 + odd * 8
+                    for pair in range(4):
+                        at = panel * 128 + pair * 32 + odd * 8
                         both = jnp.concatenate(
                             [ug[r, at : at + 8, cols], ug[r, at + 16 : at + 24, cols]], axis=0
                         )
                         above, below = split(both * keep)
-                        to = slice(pair * 16, pair * 16 + 16)
+                        to = pl.ds(pl.multiple_of(r * 64 + pair * 16, 16), 16)
                         uh[panel * 2 + odd, to, cols] = above
                         ul[panel * 2 + odd, to, cols] = below
             keep = scale(fub_ref, col * 2 + half)
-            for r in range(ROWS):
-                above, below = split(ug[r, PANELS * 128 :, cols] * keep)
-                uh[TILES - 1, r * 64 : r * 64 + 64, cols] = above
-                ul[TILES - 1, r * 64 : r * 64 + 64, cols] = below
+            above, below = split(ug[r, PANELS * 128 :, cols] * keep)
+            to = pl.ds(pl.multiple_of(r * 64, 64), 64)
+            uh[TILES - 1, to, cols] = above
+            ul[TILES - 1, to, cols] = below
 
     def compute(c, r):
         at = row * BLOCKS + c * R + r
@@ -207,25 +235,40 @@
         for q in range(TILES):
             t = tab_ref[T_OF + q, at]
             total = total - contract(high[t], low[t], uh[q], ul[q])
-        mine[c, r * BLK : r * BLK + BLK, :] = total
-
-    def upper(c):
+        mine[c * R + r] = total
+
+    def upper_near(c):
         @pl.when(c == 0)
         def _():
             load_anc.wait()
-            prepare_upper()
+            convert_upper(row)
+            u_arrive(0, sib)
+            convert_upper(sib)
+
+    def upper_far(c):
+        @pl.when(c == 0)
+        def _():
+            u_arrive(1, far)
+            u_fwd.start()
+            convert_upper(far)
+
+    def upper_last(c):
+        @pl.when(c == 0)
+        def _():
+            u_arrive(2, far_sib)
+            convert_upper(far_sib)
 
     def work(c):
         unpack(c)
         for r in range(R):
             compute(c, r)
-        exchange(c).start()
-        store_out(c).start()
+            exchange(c * R + r).start()
+            store_out(c * R + r).start()
 
     def clear(c):
         sent(a1, c, 4)
         sent(b1, c, 2)
-        sent(a2, c, 2)
+        a2_sent(c)
         sent(b2, c, 4)
 
     def starts(what):
@@ -244,13 +287,15 @@
                 for action in actions:
                     action(i - offset)
 
-        run(0, place, starts(a1), starts(b1))
-        run(1, moves(a1, 1), moves(b1, 1))
-        run(2, moves(a1, 2), ends(b1, 2), starts(b2))
-        run(3, moves(a1, 3), moves(b2, 1))
-        run(4, ends(a1, 4), starts(a2), moves(b2, 2))
-        run(5, moves(a2, 1), moves(b2, 3))
-        run(6, upper, ends(a2, 2), ends(b2, 4), work)
+        run(0, place, starts(a1), starts(b1), spread(0))
+        run(1, moves(a1, 1), moves(b1, 1), spread(1, -1))
+        run(2, moves(a1, 2), ends(b1, 2), starts(b2), spread(2, -2))
+        run(2, upper_near)
+        run(3, moves(a1, 3), moves(b2, 1), spread(3, -3))
+        run(4, ends(a1, 4), spread(4), moves(b2, 2))
+        run(4, upper_far)
+        run(5, a2_on, moves(b2, 3))
+        run(6, upper_last, a2_end, ends(b2, 4), work)
         run(7, clear)
         return 0
 
@@ -264,7 +309,7 @@
         store_out(c).wait()
         return 0
 
-    lax.fori_loop(0, chunks, drain, 0)
+    lax.fori_loop(0, BLOCKS, drain, 0)
 
 
 def tables(lb_ref, flb_ref, tab_ref, mask, other, sent, came):
@@ -333,26 +378,15 @@
     tab_ref[MOST + 1 :, :] = jnp.zeros((16 - MOST - 1, BLK), jnp.int32)
 
 
-def combine(tab_ref, mine_ref, rx_ref, out_ref, mine, rx, total, sem_m, sem_r, sem_o):
+def combine(tab_ref, mine_ref, rx_ref, out_ref, total, sem_o):
     row = lax.axis_index("row")
-
-    def loads(n):
-        at = row * BLOCKS + n
-        return (
-            pltpu.make_async_copy(mine_ref.at[tab_ref[POS, at]], mine.at[n], sem_m.at[n]),
-            pltpu.make_async_copy(rx_ref.at[tab_ref[POS_OTHER, at]], rx.at[n], sem_r.at[n]),
-        )
 
     def store(n):
         return pltpu.make_async_copy(total.at[n], out_ref.at[n], sem_o.at[n])
 
     for n in range(BLOCKS):
-        for load in loads(n):
-            load.start()
-    for n in range(BLOCKS):
-        for load in loads(n):
-            load.wait()
-        total[n] = mine[n] + rx[n]
+        at = row * BLOCKS + n
+        total[n] = mine_ref[tab_ref[POS, at]] + rx_ref[tab_ref[POS_OTHER, at]]
         store(n).start()
     for n in range(BLOCKS):
         store(n).wait()
@@ -366,7 +400,7 @@
 def gather_update(n, cols, rows):
     tiles, tiles_a = SIZES[n]
     dma = pltpu.SemaphoreType.DMA
-    result = jax.ShapeDtypeStruct((CHUNKS, R * BLK, cols), F32)
+    result = jax.ShapeDtypeStruct((BLOCKS, BLK, cols), F32)
     return pl.pallas_call(
         functools.partial(kernel, tiles, tiles_a),
         out_shape=(result, result),
@@ -381,14 +415,14 @@
             pltpu.VMEM((TILES, 256, cols), BF16),
             pltpu.VMEM((TILES, 256, cols), BF16),
             pltpu.VMEM((BLOCKS, BLK, cols), F32),
-            pltpu.VMEM((CHUNKS, R * BLK, cols), F32),
+            pltpu.VMEM((BLOCKS, BLK, cols), F32),
             dma((CHUNKS, 8)), dma((CHUNKS, 8)),
-            dma((CHUNKS, 4)), dma((CHUNKS, 4)),
+            dma((CHUNKS, 18)), dma((CHUNKS, 18)),
             dma((CHUNKS, 4)), dma((CHUNKS, 4)),
             dma((CHUNKS, 8)), dma((CHUNKS, 8)),
             dma((3,)), dma((3,)),
-            dma((CHUNKS,)), dma((CHUNKS,)),
-            dma, dma((CHUNKS,)),
+            dma((BLOCKS,)), dma((BLOCKS,)),
+            dma, dma((BLOCKS,)),
         ],
         compiler_params=pltpu.CompilerParams(
             collective_id=n + 1, has_side_effects=True, vmem_limit_bytes=56 << 20
@@ -420,12 +454,12 @@
     out = pl.pallas_call(
         combine,
         out_shape=jax.ShapeDtypeStruct(blocks, F32),
-        in_specs=[SMEM, HBM, HBM],
+        in_specs=[SMEM, VMEM, VMEM],
         out_specs=HBM,
-        scratch_shapes=[pltpu.VMEM(blocks, F32)] * 3 + [dma((BLOCKS,))] * 3,
+        scratch_shapes=[pltpu.VMEM(blocks, F32), dma((BLOCKS,))],
         compiler_params=pltpu.CompilerParams(vmem_limit_bytes=16 << 20),
         name="layer_sum",
-    )(tab, mine.reshape(blocks), rx.reshape(blocks))
+    )(tab, mine, rx)
     return out.reshape(rows, cols)
 
 

time: 116 us -> 106 us (0.914); the launches traced: 114 us -> 106 us
  Pallas kernels: 113 us -> 104 us
    pallas_call x1, Pallas kernels: 7.92 us -> 3.07 us  [body(): pl.pallas_call(combine, out_shape=jax.ShapeDtypeStruct(blocks, F32), in_s...]
    pallas_call x1, Pallas kernels: 100 us -> 96 us  [body(): lax.switch(size, [gather_update(n, cols, rows) for n in range(len(SIZES))...]
where the time goes in v4:
time: 106 us
  Pallas kernels  104 us (98%)
  between operations  1.5 us (1%)
    pallas_call x1, Pallas kernels, body(): lax.switch(size, [gather_update(n, cols, rows) for n in range(len(SIZES))...  96 us
    pallas_call x1, Pallas kernels, body(): pl.pallas_call(tables, out_shape=jax.ShapeDtypeStruct((16, BLK), jnp.int3...  4.51 us
    pallas_call x1, Pallas kernels, body(): pl.pallas_call(combine, out_shape=jax.ShapeDtypeStruct(blocks, F32), in_s...  3.07 us

profile of v4, /device:TPU:4, one launch (start us, length us, event | category | flops | bytes accessed | tf_op | source)
XLA Modules:
  0.0 105.8 jit_solution(5682622074448998051)
XLA Ops:
  0.0 4.5 %block_tables.1.tab_ref = s32[16,128]{1,0:T(8,128)S(1)} custom-call(s32[1,4,64]{2,1,0:T(4,128)} %lb_ref.1, s32[1,64]{1,0:T(1,128)} %bitcast.11), custom_call_target="tpu_custom_call" | custom-call | tf_op jit(solution)/shard_map/block_tables/pallas_call | solution.py:437
  4.5 0.5 slice.3
  6.3 96.2 %conditional.1 = ((f32[16,128,256]{2,1,0:T(8,128)S(1)}, f32[16,128,256]{2,1,0:T(8,128)})) conditional(s32[]{:T(128)} %bitcast.1, (s32[16,128]{1,0:T(8,128)S(1)}, f32[16,128,256]{2,1,0:T(8,128)}, f32[8,8,2048]{2,1,0:T(8,128)}, f32[1,4,128,256]{3,2,1,0:T(8,128)}, s32[1,4,64]{2,1,0:T(4,128)}, /*index=5*/f32[8,2048]{1,0:T(8,128)}, ...), branch_computations={%region_0.0_spmd, %region_1.0_spmd, %region_2.0_spmd} | conditional | bytes 8 | solution.py:448
  6.3 96.0 %gather_update_exchange.3 = (f32[16,128,256]{2,1,0:T(8,128)S(1)}, f32[16,128,256]{2,1,0:T(8,128)}) custom-call(s32[16,128]{1,0:T(8,128)S(1)} %get-tuple-element.53.tab_ref, f32[16,128,256]{2,1,0:T(8,128)} %get-tuple-element.54.anc_ref, f32[8,8,2048]{2,1,0:T(8,128)} %get-tuple-element.55.low_ref, f32[1,4,128,256]{3,2,1,0:T(8,128)} %get-tuple-element.56.up_ref, ...), custom_call_target="tpu_custom_call" | custom-call | tf_op jit(solution)/shard_map/cond/branch_0_fun/gather_update_exchange/pallas_call | solution.py:448
  102.5 3.1 %layer_sum.1 = f32[16,128,256]{2,1,0:T(8,128)} custom-call(s32[16,128]{1,0:T(8,128)S(1)} %block_tables.1.tab_ref, f32[16,128,256]{2,1,0:T(8,128)S(1)} %get-tuple-element.79.mine_ref, f32[16,128,256]{2,1,0:T(8,128)} %get-tuple-element.80.rx_ref), custom_call_target="tpu_custom_call" | custom-call | tf_op jit(solution)/shard_map/layer_sum/pallas_call | solution.py:454

commit v5 on v4

--- a/solution.py
+++ b/solution.py
@@ -15,8 +15,8 @@
 CHUNKS = 8
 TILES = 9
 BLOCKS = 16
-SIZES = ((11, 7), (12, 7), (18, 11))
-T_OF, ORDER, SOURCE, POS, POS_OTHER, MOST = 0, 9, 10, 12, 13, 14
+SIZES = ((10, 6), (11, 7), (12, 7), (18, 11))
+T_OF, ORDER, SOURCE, POS, POS_OTHER = 0, 9, 10, 12, 13
 MESH = pl.DeviceIdType.MESH
 F32, BF16 = jnp.float32, jnp.bfloat16
 
@@ -26,18 +26,20 @@
     return high, (value - high.astype(F32)).astype(BF16)
 
 
-def contract(high, low, upper_high, upper_low):
+def contract(high, low, upper, q):
+    cols = upper.shape[2] // 2
 
     def dot(a, b):
         return lax.dot_general(a, b, (((0,), (0,)), ((), ())), preferred_element_type=F32)
 
-    return dot(high, upper_high) + dot(high, upper_low) + dot(low, upper_high)
+    both = dot(high, upper[q])
+    return both[:, :cols] + both[:, cols:] + dot(low, upper[q, :, :cols])
 
 
 def kernel(
     tiles, tiles_a, tab_ref, anc_ref, low_ref, up_ref, ub_ref, fl_ref, fu_ref, fub_ref,
     mine_ref, rx_ref,
-    gathered, own, high, low, ug, uh, ul, anc, mine,
+    gathered, own, high, low, ug, upper, anc, mine,
     s_a1, r_a1, s_a2, r_a2, s_b1, r_b1, s_b2, r_b2, s_u, r_u, s_x, r_x, l_anc, l_out,
 ):
     chunks = CHUNKS
@@ -211,6 +213,7 @@
     def convert_upper(r):
         for half in range(2):
             cols = slice(half * BLK, half * BLK + BLK)
+            beside = slice((2 + half) * BLK, (3 + half) * BLK)
             for panel in range(PANELS):
                 keep = scale(ub_ref, 0, panel, col * 2 + half)
                 for odd in range(2):
@@ -221,20 +224,20 @@
                         )
                         above, below = split(both * keep)
                         to = pl.ds(pl.multiple_of(r * 64 + pair * 16, 16), 16)
-                        uh[panel * 2 + odd, to, cols] = above
-                        ul[panel * 2 + odd, to, cols] = below
+                        upper[panel * 2 + odd, to, cols] = above
+                        upper[panel * 2 + odd, to, beside] = below
             keep = scale(fub_ref, col * 2 + half)
             above, below = split(ug[r, PANELS * 128 :, cols] * keep)
             to = pl.ds(pl.multiple_of(r * 64, 64), 64)
-            uh[TILES - 1, to, cols] = above
-            ul[TILES - 1, to, cols] = below
+            upper[TILES - 1, to, cols] = above
+            upper[TILES - 1, to, beside] = below
 
     def compute(c, r):
         at = row * BLOCKS + c * R + r
         total = anc[tab_ref[ORDER, at]]
         for q in range(TILES):
             t = tab_ref[T_OF + q, at]
-            total = total - contract(high[t], low[t], uh[q], ul[q])
+            total = total - contract(high[t], low[t], upper, q)
         mine[c * R + r] = total
 
     def upper_near(c):
@@ -312,7 +315,7 @@
     lax.fori_loop(0, BLOCKS, drain, 0)
 
 
-def tables(lb_ref, flb_ref, tab_ref, mask, other, sent, came):
+def tables(lb_ref, flb_ref, tab_ref, size_ref, mask, other, sent, came):
     layer = lax.axis_index("layer")
     row = lax.axis_index("row")
     barrier = pltpu.get_barrier_semaphore()
@@ -371,11 +374,15 @@
     copy.wait()
     place_other, _, most_other = ranked(other[...])
     out.append(place_other)
-    out.append(jnp.broadcast_to(jnp.maximum(most, most_other), (1, BLK)))
+    most = jnp.max(jnp.maximum(most, most_other)).astype(jnp.int32)
+    size = jnp.int32(0)
+    for tiles, _ in SIZES[:-1]:
+        size = size + (most > tiles * CHUNKS).astype(jnp.int32)
+    size_ref[0] = size
     tab_ref[0:TILES + 1, :] = (moved[0:TILES + 1] + 0.5).astype(jnp.int32)
     for n, value in enumerate(out):
         tab_ref[SOURCE + n : SOURCE + n + 1, :] = value.astype(jnp.int32)
-    tab_ref[MOST + 1 :, :] = jnp.zeros((16 - MOST - 1, BLK), jnp.int32)
+    tab_ref[POS_OTHER + 1 :, :] = jnp.zeros((15 - POS_OTHER, BLK), jnp.int32)
 
 
 def combine(tab_ref, mine_ref, rx_ref, out_ref, total, sem_o):
@@ -412,8 +419,7 @@
             pltpu.VMEM((CHUNKS * tiles + 1, 256, BLK), BF16),
             pltpu.VMEM((CHUNKS * tiles + 1, 256, BLK), BF16),
             pltpu.VMEM((ROWS, PANELS * 128 + 64, cols), F32),
-            pltpu.VMEM((TILES, 256, cols), BF16),
-            pltpu.VMEM((TILES, 256, cols), BF16),
+            pltpu.VMEM((TILES, 256, 2 * cols), BF16),
             pltpu.VMEM((BLOCKS, BLK, cols), F32),
             pltpu.VMEM((BLOCKS, BLK, cols), F32),
             dma((CHUNKS, 8)), dma((CHUNKS, 8)),
@@ -434,19 +440,19 @@
 def body(anc, low, up, lb, ub, fl, fu, flb, fub):
     rows, cols = anc.shape[1:]
     dma = pltpu.SemaphoreType.DMA
-    tab = pl.pallas_call(
+    tab, size = pl.pallas_call(
         tables,
-        out_shape=jax.ShapeDtypeStruct((16, BLK), jnp.int32),
+        out_shape=(
+            jax.ShapeDtypeStruct((16, BLK), jnp.int32), jax.ShapeDtypeStruct((1,), jnp.int32)
+        ),
         in_specs=[VMEM, VMEM],
-        out_specs=VMEM,
+        out_specs=(VMEM, SMEM),
         scratch_shapes=[pltpu.VMEM((8, BLK), F32), pltpu.VMEM((8, BLK), F32), dma, dma],
         compiler_params=pltpu.CompilerParams(collective_id=0, has_side_effects=True),
         name="block_tables",
     )(lb, flb.reshape(1, -1))
-    most = tab[MOST, 0]
-    size = sum((most > tiles * CHUNKS).astype(jnp.int32) for tiles, _ in SIZES[:-1])
     mine, rx = lax.switch(
-        size,
+        size[0],
         [gather_update(n, cols, rows) for n in range(len(SIZES))],
         tab, anc.reshape(BLOCKS, BLK, cols), low.reshape(2 * PANELS, 8, rows), up, ub, fl, fu, fub,
     )

time: 106 us -> 104 us (0.981); the launches traced: 106 us -> 101 us
  Pallas kernels: 104 us -> 100 us
    pallas_call x2, Pallas kernels: 100 us -> 97.3 us  [the longest x1 92.2 us: body(): lax.switch(size[0], [gather_update(n, cols, rows) for n in range(len(SIZE...]
where the time goes in v5:
time: 104 us; the launch traced here: 101 us
  Pallas kernels  100 us (96%)
    pallas_call x1, Pallas kernels, body(): lax.switch(size[0], [gather_update(n, cols, rows) for n in range(len(SIZE...  92.2 us
    pallas_call x1, Pallas kernels, body(): pl.pallas_call(tables, out_shape=(jax.ShapeDtypeStruct((16, BLK), jnp.int...  5.06 us
    pallas_call x1, Pallas kernels, body(): pl.pallas_call(combine, out_shape=jax.ShapeDtypeStruct(blocks, F32), in_s...  3.07 us

profile of v5, /device:TPU:4, one launch (start us, length us, event | category | flops | bytes accessed | tf_op | source)
XLA Modules:
  0.0 101.5 jit_solution(16205582606516439649)
XLA Ops:
  0.0 5.1 %block_tables.1 = (s32[16,128]{1,0:T(8,128)S(1)}, s32[1]{0:T(128)}) custom-call(s32[1,4,64]{2,1,0:T(4,128)} %lb_ref.1, s32[1,64]{1,0:T(1,128)} %bitcast.13), custom_call_target="tpu_custom_call" | custom-call | tf_op jit(solution)/shard_map/block_tables/pallas_call | solution.py:443
  5.8 92.5 %conditional.1 = ((f32[16,128,256]{2,1,0:T(8,128)S(1)}, f32[16,128,256]{2,1,0:T(8,128)})) conditional(s32[]{:T(128)} %bitcast.1, (s32[16,128]{1,0:T(8,128)S(1)}, f32[16,128,256]{2,1,0:T(8,128)}, f32[8,8,2048]{2,1,0:T(8,128)}, f32[1,4,128,256]{3,2,1,0:T(8,128)}, s32[1,4,64]{2,1,0:T(4,128)}, ...), branch_computations={%region_0.0_spmd, %region_1.0_spmd, %region_2.0_spmd, %region_3.0_... | conditional | bytes 8 | solution.py:454
  5.8 92.2 %gather_update_exchange.4 = (f32[16,128,256]{2,1,0:T(8,128)S(1)}, f32[16,128,256]{2,1,0:T(8,128)}) custom-call(s32[16,128]{1,0:T(8,128)S(1)} %get-tuple-element.69.tab_ref, f32[16,128,256]{2,1,0:T(8,128)} %get-tuple-element.70.anc_ref, f32[8,8,2048]{2,1,0:T(8,128)} %get-tuple-element.71.low_ref, f32[1,4,128,256]{3,2,1,0:T(8,128)} %get-tuple-element.72.up_ref, ...), custom_call_target="tpu_custom_call" | custom-call | tf_op jit(solution)/shard_map/cond/branch_0_fun/gather_update_exchange/pallas_call | solution.py:454
  98.2 3.1 %layer_sum.1 = f32[16,128,256]{2,1,0:T(8,128)} custom-call(s32[16,128]{1,0:T(8,128)S(1)} %get-tuple-element.105.tab_ref, f32[16,128,256]{2,1,0:T(8,128)S(1)} %get-tuple-element.107.mine_ref, f32[16,128,256]{2,1,0:T(8,128)} %get-tuple-element.108.rx_ref), custom_call_target="tpu_custom_call" | custom-call | tf_op jit(solution)/shard_map/layer_sum/pallas_call | solution.py:460

commit v6 on v5

--- a/solution.py
+++ b/solution.py
@@ -15,7 +15,7 @@
 CHUNKS = 8
 TILES = 9
 BLOCKS = 16
-SIZES = ((10, 6), (11, 7), (12, 7), (18, 11))
+SIZES = ((10, 6), (11, 7), (12, 7), (14, 8), (18, 11))
 T_OF, ORDER, SOURCE, POS, POS_OTHER = 0, 9, 10, 12, 13
 MESH = pl.DeviceIdType.MESH
 F32, BF16 = jnp.float32, jnp.bfloat16

time: 104 us -> 103 us (level)
  no operation moved by 1% of the time
where the time goes in v6:
time: 103 us; the launch traced here: 101 us
  Pallas kernels  100 us (97%)
    pallas_call x1, Pallas kernels, body(): lax.switch(size[0], [gather_update(n, cols, rows) for n in range(len(SIZE...  92.2 us
    pallas_call x1, Pallas kernels, body(): pl.pallas_call(tables, out_shape=(jax.ShapeDtypeStruct((16, BLK), jnp.int...  5.06 us
    pallas_call x1, Pallas kernels, body(): pl.pallas_call(combine, out_shape=jax.ShapeDtypeStruct(blocks, F32), in_s...  3.07 us

profile of v6, /device:TPU:4, one launch (start us, length us, event | category | flops | bytes accessed | tf_op | source)
XLA Modules:
  0.0 101.4 jit_solution(7499767084880277020)
XLA Ops:
  0.0 5.1 %block_tables.1 = (s32[16,128]{1,0:T(8,128)S(1)}, s32[1]{0:T(128)}) custom-call(s32[1,4,64]{2,1,0:T(4,128)} %lb_ref.1, s32[1,64]{1,0:T(1,128)} %bitcast.15), custom_call_target="tpu_custom_call" | custom-call | tf_op jit(solution)/shard_map/block_tables/pallas_call | solution.py:443
  5.6 92.5 %conditional.1 = ((f32[16,128,256]{2,1,0:T(8,128)S(1)}, f32[16,128,256]{2,1,0:T(8,128)})) conditional(s32[]{:T(128)} %bitcast.1, (s32[16,128]{1,0:T(8,128)S(1)}, f32[16,128,256]{2,1,0:T(8,128)}, f32[8,8,2048]{2,1,0:T(8,128)}, f32[1,4,128,256]{3,2,1,0:T(8,128)}, s32[1,4,64]{2,1,0:T(4,128)}, ...), branch_computations={%region_0.0_spmd, %region_1.0_spmd, %region_2.0_spmd, %region_3.0_... | conditional | bytes 8 | solution.py:454
  5.6 92.2 %gather_update_exchange.5 = (f32[16,128,256]{2,1,0:T(8,128)S(1)}, f32[16,128,256]{2,1,0:T(8,128)}) custom-call(s32[16,128]{1,0:T(8,128)S(1)} %get-tuple-element.85.tab_ref, f32[16,128,256]{2,1,0:T(8,128)} %get-tuple-element.86.anc_ref, f32[8,8,2048]{2,1,0:T(8,128)} %get-tuple-element.87.low_ref, f32[1,4,128,256]{3,2,1,0:T(8,128)} %get-tuple-element.88.up_ref, ...), custom_call_target="tpu_custom_call" | custom-call | tf_op jit(solution)/shard_map/cond/branch_0_fun/gather_update_exchange/pallas_call | solution.py:454
  98.1 3.1 %layer_sum.1 = f32[16,128,256]{2,1,0:T(8,128)} custom-call(s32[16,128]{1,0:T(8,128)S(1)} %get-tuple-element.129.tab_ref, f32[16,128,256]{2,1,0:T(8,128)S(1)} %get-tuple-element.131.mine_ref, f32[16,128,256]{2,1,0:T(8,128)} %get-tuple-element.132.rx_ref), custom_call_target="tpu_custom_call" | custom-call | tf_op jit(solution)/shard_map/layer_sum/pallas_call | solution.py:460
